TPU v7x, 32 devices: a whole 2x2x4 slice. The times are simulated.
32 devices in a mesh: groups: 2 (over y), seq: 4 (over z), clus: 2 (over x), dp: 2 (over core).
Axes of the slice: x: 2, y: 2, z: 4, core: 2. Of those that a mesh axis runs over, the one named last changes fastest.
Arguments:
- layer_input: bfloat16 [4, 2048, 2048], P(('groups', 'dp'), 'seq'), parts along dimension 0, may hold values from -6 to 6
- queries: bfloat16 [4, 2048, 1024], P(('groups', 'dp'), 'seq', 'clus'), parts along dimension 0, may hold values from -18 to 18
- keys: bfloat16 [4, 2048, 1024], P(('groups', 'dp'), 'seq', 'clus'), parts along dimension 0, may hold values from -18 to 18
- values: bfloat16 [4, 2048, 1024], P(('groups', 'dp'), 'seq', 'clus'), parts along dimension 0, may hold values from -6 to 6
- out_grad: bfloat16 [4, 2048, 1024], P(('groups', 'dp'), 'seq', 'clus'), parts along dimension 0, may hold values from -6 to 6
- cluster_ids: int32 [4, 8, 2048], P(('groups', 'dp'), 'clus', 'seq'), parts along dimension 0, may hold values from 0 to 3
- slots: int32 [4, 8, 2048], P(('groups', 'dp'), 'clus', 'seq'), parts along dimension 0, may hold values from -1 to 1023, as said below
- counts: int32 [4, 8, 4, 4], P(('groups', 'dp'), 'clus', 'seq'), parts along dimension 0, may hold values from 0 to 256, as said below
Outputs:
- query_grad: bfloat16 [4, 2048, 1024], P(('groups', 'dp'), 'seq', 'clus'), parts along dimension 0
- key_grad: bfloat16 [4, 2048, 1024], P(('groups', 'dp'), 'seq', 'clus'), parts along dimension 0
- value_grad: bfloat16 [4, 2048, 1024], P(('groups', 'dp'), 'seq', 'clus'), parts along dimension 0
- weight_grad: float32 [4096, 3, 1024], P(('groups', 'seq'), None, 'clus'), parts along dimension 0
- centroid_dirs: float32 [16, 4, 128], P(('groups', 'clus'), 'seq'), parts along dimension 0
There are 2 independent parts, one for each index of `groups`. A program takes and returns all parts, laid end to end along the dimension named above; each array names one. Nothing has to cross between parts.
Inputs may be any that keep to these rules, and one draw needn't show every extreme that they name: `slots`: -1 marks a token left out of its cluster; otherwise the slot is s * 256 + r, where s is the index along seq of the device that holds the token and r counts the earlier kept tokens of that device with the same cluster and head, so at most 256 tokens of one device are kept in one cluster; in every head of every clip some cluster keeps 256 tokens from every device. counts[b, h, j, s] is the number of tokens of device s kept in cluster j of head h, the same as given by slots.
All inputs are finite; a program needn't handle non-finite values.
Results may differ from a plain program's by a relative error of at most 0.012.
The roundings to bfloat16 on the way count: a program that leaves them out, or rounds other values in their place, can miss the bound.
Values may be sent and summed in bfloat16 or wider, within the bound.
A program may use at most 64 MiB of HBM per device.

v0:
```python
import jax
import jax.numpy as jnp
from jax import lax
from jax.sharding import PartitionSpec as P

CAP = 1024


def for_sending(value):
    return jax.tree.map(lambda a: a.astype(jnp.bfloat16) if a.dtype == jnp.float32 else a, value)


def contract_rows(left, right):
    return lax.dot_general(
        left, right, (((0,), (0,)), ((), ())), preferred_element_type=jnp.float32
    )


def contract_cols(left, right):
    return lax.dot_general(
        left, right, (((1,), (1,)), ((), ())), preferred_element_type=jnp.float32
    )


def unit_rows(array):
    wide = array.astype(jnp.float32)
    return wide * lax.rsqrt(jnp.mean(wide * wide, axis=-1, keepdims=True) + 1e-06)


def block_backward(block, live, rows):
    width = block.shape[1] // 4
    scale = width ** (-0.5)
    query = block[:, :width]
    key = block[:, width : 2 * width]
    value = block[:, 2 * width : 3 * width]
    grad = block[:, 3 * width :]
    key_total = jnp.zeros((block.shape[0], width), jnp.float32)
    value_total = jnp.zeros((block.shape[0], width), jnp.float32)
    query_parts = []
    for start in range(0, block.shape[0], rows):
        query_rows = query[start : start + rows]
        grad_rows = grad[start : start + rows]
        scores = contract_cols(query_rows, key) * scale
        scores = jnp.where(live[None, :], scores, -1e30)
        top = jnp.max(scores, axis=1, keepdims=True)
        weights = jnp.exp(scores - top)
        probs = weights / jnp.sum(weights, axis=1, keepdims=True)
        probs_low = probs.astype(jnp.bfloat16)
        recomputed = jnp.dot(probs_low, value, preferred_element_type=jnp.float32)
        delta = jnp.sum(grad_rows.astype(jnp.float32) * recomputed, axis=1, keepdims=True)
        dprobs = contract_cols(grad_rows, value)
        dscores = (probs * (dprobs - delta)).astype(jnp.bfloat16)
        query_parts.append(jnp.dot(dscores, key, preferred_element_type=jnp.float32) * scale)
        key_total = key_total + contract_rows(dscores, query_rows)
        value_total = value_total + contract_rows(probs_low, grad_rows)
    query_total = jnp.concatenate(query_parts, axis=0)
    return jnp.concatenate((query_total, key_total * scale, value_total), axis=1).astype(
        jnp.bfloat16
    )


def on_device(layer_input, queries, keys, values, out_grad, cluster_ids, slots, counts):
    sources = lax.axis_size("seq")
    heads_here = cluster_ids.shape[1]
    tokens_here = queries.shape[1]
    width = queries.shape[2] // heads_here
    clusters_here = counts.shape[2]
    reserved = CAP // sources
    block_rows = clusters_here * reserved
    total_rows = sources * block_rows

    def per_head(array):
        return array[0].reshape(tokens_here, heads_here, width).transpose(1, 0, 2)

    query_heads = per_head(queries)
    key_heads = per_head(keys)
    rows = jnp.concatenate((query_heads, key_heads, per_head(values), per_head(out_grad)), axis=2)
    cluster = cluster_ids[0]
    slot = slots[0]
    kept = slot >= 0
    place = jnp.where(kept, cluster * reserved + slot % reserved, total_rows)

    def fill(row_set, spots):
        return (
            jnp.zeros((total_rows + 1, row_set.shape[1]), row_set.dtype)
            .at[spots]
            .set(row_set)[:total_rows]
        )

    outgoing = jax.vmap(fill)(rows, place).reshape(heads_here, sources, block_rows, 4 * width)
    within = jnp.arange(reserved, dtype=jnp.int32)
    live = (within[None, None, None, :] < counts[0][..., None]).reshape(
        heads_here, clusters_here, CAP
    )
    arrived = lax.all_to_all(outgoing, "seq", split_axis=1, concat_axis=1, tiled=True)
    number = arrived.shape[0]
    blocks = arrived.reshape(number, sources, clusters_here, reserved, 4 * width)
    blocks = blocks.transpose(0, 2, 1, 3, 4).reshape(number * clusters_here, CAP, 4 * width)
    flat_mask = live.reshape(number * clusters_here, CAP)
    grads = lax.map(
        lambda item: block_backward(item[0], item[1], min(CAP, 512)), (blocks, flat_mask)
    )
    home = grads.reshape(number, clusters_here, sources, reserved, 3 * width)
    home = home.transpose(0, 2, 1, 3, 4).reshape(number, sources, block_rows, 3 * width)
    unit = (unit_rows(blocks[..., :width]) + unit_rows(blocks[..., width : 2 * width])) * flat_mask[
        ..., None
    ].astype(jnp.float32)
    sums = jnp.sum(unit, axis=1).reshape(number, clusters_here, width)
    home, owner_total = (home, sums)
    returned = lax.all_to_all(
        for_sending(home), "seq", split_axis=1, concat_axis=1, tiled=True
    ).astype(home.dtype)
    padded = jnp.concatenate(
        (
            returned.reshape(heads_here, total_rows, 3 * width),
            jnp.zeros((heads_here, 1, 3 * width), returned.dtype),
        ),
        axis=1,
    )
    back = jax.vmap(lambda table, spots: table[spots])(padded, place)

    def token_major(part):
        return part.transpose(1, 0, 2).reshape(tokens_here, heads_here * width)

    query_grad = token_major(back[:, :, :width])
    key_grad = token_major(back[:, :, width : 2 * width])
    value_grad = token_major(back[:, :, 2 * width :])
    stacked = jnp.stack((query_grad, key_grad, value_grad), axis=1).reshape(
        tokens_here, 3 * heads_here * width
    )
    inputs = layer_input[0]
    weight_share = lax.psum_scatter(
        contract_rows(inputs, stacked)
        .reshape(lax.axis_size("seq") * (inputs.shape[1] // sources), 3, heads_here * width)
        .astype(jnp.bfloat16),
        "seq",
        scatter_dimension=0,
        tiled=True,
    )
    unit = (unit_rows(query_heads) + unit_rows(key_heads)) * kept[..., None].astype(jnp.float32)
    member = (cluster[..., None] == jnp.arange(sources * clusters_here, dtype=jnp.int32)).astype(
        jnp.float32
    )
    term = jnp.einsum("htc,hte->hce", member, unit, precision=lax.Precision.HIGHEST)
    centroid_part = lax.psum_scatter(
        term.astype(jnp.bfloat16), "seq", scatter_dimension=1, tiled=True
    )
    weight_grad, centroid_total = (
        lax.psum(weight_share, "dp").astype(jnp.float32),
        lax.psum(centroid_part, "dp").astype(jnp.float32),
    )
    centroid_dirs = centroid_total * lax.rsqrt(
        jnp.mean(centroid_total * centroid_total, axis=-1, keepdims=True) + 1e-06
    )
    return (query_grad[None], key_grad[None], value_grad[None], weight_grad, centroid_dirs)


def solution(mesh):
    return jax.shard_map(
        on_device,
        mesh=mesh,
        in_specs=(
            P(("groups", "dp"), "seq", None),
            P(("groups", "dp"), "seq", "clus"),
            P(("groups", "dp"), "seq", "clus"),
            P(("groups", "dp"), "seq", "clus"),
            P(("groups", "dp"), "seq", "clus"),
            P(("groups", "dp"), "clus", "seq"),
            P(("groups", "dp"), "clus", "seq"),
            P(("groups", "dp"), "clus", "seq", None),
        ),
        out_specs=(
            P(("groups", "dp"), "seq", "clus"),
            P(("groups", "dp"), "seq", "clus"),
            P(("groups", "dp"), "seq", "clus"),
            P(("groups", "seq"), None, "clus"),
            P(("groups", "clus"), "seq", None),
        ),
        check_vma=False,
    )
```

profile of v0, /device:TPU:0, one launch (start us, length us, event | category | flops | bytes accessed | tf_op | source)
XLA Modules:
  0.0 490.8 jit_solution(16918221700033991683)
XLA Ops:
  18.8 12.6 %scatter_custom_fusion = bf16[4100,512]{1,0:T(8,128)(2,1)} fusion(s32[2048]{0:T(1024)S(1)} %bitcast.123, bf16[2048,512]{1,0:T(8,128)(2,1)} %bitcast.119, bf16[]{:T(256)} %constant.25.clone.1), kind=kCustom, calls=%fused_computation.58 | custom fusion | bytes 4198912
  31.3 7.9 %reshape.211 = bf16[1025,4,512]{2,1,0:T(4,128)(2,1)} reshape(bf16[4100,512]{1,0:T(8,128)(2,1)} %scatter_custom_fusion) | data formatting | bytes 8396800
  39.2 5.6 %slice.48 = bf16[4,1024,512]{2,0,1:T(4,128)(2,1)} slice(bf16[4,1025,512]{2,0,1:T(4,128)(2,1)} %bitcast.108), slice={[0:4], [0:1024], [0:512]} | slice | bytes 8388608 | tf_op jit(solution)/shard_map/vmap()/slice | solution.py:85
  44.8 6.5 %all-to-all-start = ((bf16[4,4,256,512]{3,0,2,1:T(4,128)(2,1)}), bf16[4,4,256,512]{3,0,2,1:T(4,128)(2,1)}, u32[]{:S(2)}, u32[]{:S(2)}) async-start(bf16[4,4,256,512]{3,0,2,1:T(4,128)(2,1)} %bitcast.109), calls=%async_computation | async-start | bytes 8388608 | tf_op jit(solution)/shard_map/all_to_all | solution.py:95
  51.4 93.5 %all-to-all-done = bf16[4,4,256,512]{3,0,2,1:T(4,128)(2,1)} async-done(((bf16[4,4,256,512]{3,0,2,1:T(4,128)(2,1)}), bf16[4,4,256,512]{3,0,2,1:T(4,128)(2,1)}, u32[]{:S(2)}, u32[]{:S(2)}) %all-to-all-start) | async-done | bytes 4194336 | tf_op jit(solution)/shard_map/all_to_all | solution.py:95
  144.8 7.5 %copy.66 = bf16[4,1024,512]{1,2,0:T(8,128)(2,1)} copy(bf16[4,1024,512]{2,0,1:T(4,128)(2,1)} %bitcast.14) | data formatting | bytes 8388608 | tf_op jit(solution)/shard_map/reshape;transpose;reshape | solution.py:98
  152.3 42.3 %while.10 = (s32[]{:T(128)}, bf16[4,1024,384]{2,1,0:T(8,128)(2,1)}, pred[4,1024]{1,0:T(4,128)(4,1)S(1)}, bf16[4,1024,512]{1,2,0:T(8,128)(2,1)}, s32[]{:T(128)}) while((s32[]{:T(128)}, bf16[4,1024,384]{2,1,0:T(8,128)(2,1)}, pred[4,1024]{1,0:T(4,128)(4,1)S(1)}, bf16[4,1024,512]{1,2,0:T(8,128)(2,1)}, s32[]{:T(128)}) %tuple.40), condition=%wide.region_8.9_spmd, body=%wide.region_1.8_spmd.sunk | while | flops 1631581184 | bytes 48268368 | solution.py:100
  194.6 6.0 %copy.52 = bf16[4,4,256,384]{3,0,2,1:T(4,128)(2,1)} copy(bf16[4,4,256,384]{3,2,1,0:T(8,128)(2,1)} %bitcast.118) | data formatting | bytes 6291456 | tf_op jit(solution)/shard_map/reshape;transpose;reshape | solution.py:104
  200.6 4.6 all-to-all-start.1
  205.5 70.0 %all-to-all-done.1 = bf16[4,4,256,384]{3,0,2,1:T(4,128)(2,1)} async-done(((bf16[4,4,256,384]{3,0,2,1:T(4,128)(2,1)}), bf16[4,4,256,384]{3,0,2,1:T(4,128)(2,1)}, u32[]{:S(2)}, u32[]{:S(2)}) %all-to-all-start.1) | async-done | bytes 3145760 | tf_op jit(solution)/shard_map/all_to_all | solution.py:110
  275.5 5.0 %concatenate.28 = bf16[4,1025,384]{2,0,1:T(4,128)(2,1)} pad(bf16[4,1024,384]{2,0,1:T(4,128)(2,1)} %bitcast.16, bf16[]{:T(256)} %constant.25.clone.1), padding=0_0x0_1x0_0 | pad | bytes 6294530 | tf_op jit(solution)/shard_map/concatenate | solution.py:113
  280.5 41.5 %gather_fusion = bf16[2048,384]{1,0:T(8,128)(2,1)} fusion(bf16[4,1025,384]{2,0,1:T(4,128)(2,1)} %concatenate.28, s32[2048]{0:T(1024)S(1)} %bitcast.107), kind=kCustom, calls=%fused_computation | custom fusion | bytes 3162112 | tf_op jit(solution)/shard_map/vmap()/gather | solution.py:120
  322.0 2.5 fusion.55
  324.6 2.1 copy.69
  326.6 2.0 copy.68
  328.7 2.0 copy.67
  332.3 5.3 %convolution_convert_fusion = bf16[1536,2048]{1,0:T(8,128)(2,1)} fusion(bf16[512,1536]{0,1:T(8,128)(2,1)S(1)} %bitcast.120, bf16[1,512,2048]{2,1,0:T(8,128)(2,1)S(1)} %copy-done), kind=kOutput, calls=%fused_computation.57 | convolution fusion | flops 3224371200 | bytes 9961472 | tf_op jit(solution)/shard_map/dot_general | solution.py:14
  337.6 8.6 %copy.56 = bf16[2048,3,512]{2,0,1:T(8,128)(2,1)} copy(bf16[2048,3,512]{0,2,1:T(8,128)(2,1)} %bitcast.110) | data formatting | bytes 12582912 | tf_op jit(solution)/shard_map/convert_element_type | solution.py:135
  346.3 110.8 %reduce-scatter.2.cloned.1.call-done = bf16[512,3,512]{2,0,1:T(8,128)(2,1)} async-done(((bf16[2048,3,512]{2,0,1:T(8,128)(2,1)}), bf16[512,3,512]{2,0,1:T(8,128)(2,1)}) %reduce-scatter.2.cloned.1.call-update) | async-done | bytes 1572880 | tf_op jit(solution)/shard_map/reduce_scatter | solution.py:132
  459.9 10.9 %all-reduce.1 = bf16[4,4,128]{2,0,1:T(4,128)(2,1)S(1)} all-reduce(bf16[4,4,128]{2,0,1:T(4,128)(2,1)S(1)} %copy.57), channel_id=3, replica_groups=mesh['groups'=2,'seq'=4,'clus'=2,'dp'=2] {'seq'}, use_global_device_ids=true, to_apply=%region_13.14.clone | all-reduce | flops 2048 | bytes 8192
  471.5 2.5 psum.15
  474.7 2.1 copy.58
  476.8 2.1 copy.59
  480.4 3.5 convert_element_type.65
  (126 shorter events, 61.2 us)
Async XLA Ops:
  7.2 325.1 %copy-start = (bf16[1,512,2048]{2,1,0:T(8,128)(2,1)S(1)}, bf16[1,512,2048]{2,1,0:T(8,128)(2,1)}, u32[]{:S(2)}) copy-start(bf16[1,512,2048]{2,1,0:T(8,128)(2,1)} %param.10) | copy-start | bytes 6291460
  15.8 1.0 copy-start.2
  15.9 1.2 copy-start.3
  44.8 6.5 %copy-start.6 = (s32[1,4,1,4]{3,2,1,0:T(1,128)S(1)}, s32[1,4,1,4]{3,2,1,0:T(1,128)}, u32[]{:S(2)}) copy-start(s32[1,4,1,4]{3,2,1,0:T(1,128)} %param.17) | copy-start | bytes 196
  44.8 100.1 %all-to-all-start = ((bf16[4,4,256,512]{3,0,2,1:T(4,128)(2,1)}), bf16[4,4,256,512]{3,0,2,1:T(4,128)(2,1)}, u32[]{:S(2)}, u32[]{:S(2)}) async-start(bf16[4,4,256,512]{3,0,2,1:T(4,128)(2,1)} %bitcast.109), calls=%async_computation | async-start | bytes 8388608 | tf_op jit(solution)/shard_map/all_to_all | solution.py:95
  200.6 74.9 %all-to-all-start.1 = ((bf16[4,4,256,384]{3,0,2,1:T(4,128)(2,1)}), bf16[4,4,256,384]{3,0,2,1:T(4,128)(2,1)}, u32[]{:S(2)}, u32[]{:S(2)}) async-start(bf16[4,4,256,384]{3,0,2,1:T(4,128)(2,1)} %copy.52), calls=%async_computation.1 | async-start | bytes 6291456 | tf_op jit(solution)/shard_map/all_to_all | solution.py:110
  205.3 251.9 %reduce-scatter.2.cloned.1.call-start = ((), (), s32[]{:S(2)}) async-start(), calls=%async_computation.3 | async-start | bytes 7864320 | tf_op jit(solution)/shard_map/reduce_scatter | solution.py:132
  346.2 111.6 %copy-start.4 = (s32[1,4,512]{2,1,0:T(4,128)S(1)}, s32[1,4,512]{2,1,0:T(4,128)}, u32[]{:S(2)}) copy-start(s32[1,4,512]{2,1,0:T(4,128)} %param.16) | copy-start | bytes 24580
  346.3 111.7 %copy-start.5 = (s32[1,4,512]{2,1,0:T(4,128)S(1)}, s32[1,4,512]{2,1,0:T(4,128)}, u32[]{:S(2)}) copy-start(s32[1,4,512]{2,1,0:T(4,128)} %param.15) | copy-start | bytes 24580
  346.3 134.1 %all-reduce.4.cloned.1.call-start = ((), (), s32[]{:S(2)}) async-start(), calls=%async_computation.4 | async-start | bytes 3145728 | tf_op jit(solution)/shard_map/psum | solution.py:149
  457.1 2.2 copy-start.7
  459.3 19.6 %copy-start.1 = (bf16[4,512,128]{1,2,0:T(8,128)(2,1)S(1)}, bf16[4,512,128]{1,2,0:T(8,128)(2,1)}, u32[]{:S(2)}) copy-start(bf16[4,512,128]{1,2,0:T(8,128)(2,1)} %copy.69) | copy-start | bytes 1572868
Sparse Core Ops, SparseCore 0:
  346.4 110.7 reduce-scatter.1
  459.5 20.8 all-reduce.3
where the time goes:
time: 493 us; the launch traced here: 491 us
  waiting for transfers between devices  275 us (56%)
  local copies, waits for them, and re-layouts  123 us (25%)
  matrix products  30.6 us (6%)
  other arithmetic  23.3 us (5%)
  between operations  14.3 us (3%)
  blocking collectives  13.4 us (3%)
  starting transfers between devices  11.4 us (2%)
    reduce_scatter x1, waiting for transfers between devices, on_device(): lax.psum_scatter(contract_rows(inputs, stacked).reshape(lax.axis_size('se...  111 us
    all_to_all x1, waiting for transfers between devices, on_device(): lax.all_to_all(outgoing, 'seq', split_axis=1, concat_axis=1, tiled=True)  93.5 us
    all_to_all x1, waiting for transfers between devices, on_device(): lax.all_to_all(for_sending(home), 'seq', split_axis=1, concat_axis=1, til...  70 us
    gather x1, local copies, waits for them, and re-layouts, on_device(): back = jax.vmap(lambda table, spots: table[spots])(padded, place)  41.5 us
    unnamed x32, local copies, waits for them, and re-layouts  34.2 us
    dot_general x17, matrix products, contract_rows(): lax.dot_general(left, right, (((0,), (0,)), ((), ())), preferred_element_...  13 us
    unnamed x1, blocking collectives  10.9 us
  transfers between devices with their start and end apart: 4, of which 4 were waited for; matrix products, arithmetic and copies ran while one was open for 2% of the time, Pallas kernels for 0%

commit v1 on v0

--- a/solution.py
+++ b/solution.py
@@ -1,9 +1,374 @@
+import functools
+
 import jax
 import jax.numpy as jnp
 from jax import lax
+from jax.experimental import pallas as pl
+from jax.experimental.pallas import tpu as pltpu
 from jax.sharding import PartitionSpec as P
 
 CAP = 1024
+MESH = pl.DeviceIdType.MESH
+LOG2E = 1.4426950408889634
+FAR = 131072.0
+
+
+def dot(left, right, left_dim, right_dim):
+    return lax.dot_general(
+        left, right, (((left_dim,), (right_dim,)), ((), ())), preferred_element_type=jnp.float32
+    )
+
+
+def exchange(
+    sources, tokens, width, model, clusters,
+    layer, queries, keys, values, grads, ids,
+    query_out, key_out, value_out, weight_out, dirs_out,
+    rows, ids_all, query_wide, key_wide, keep, probs, key_sum, value_sum, back, landed,
+    layer_rows, layer_cols, sib_term, sib_in, term, from_left, from_right, total,
+    cent_mine, cent_sib, cent_all,
+    row_send, row_recv, id_send, id_recv, local_sem, back_send, back_recv,
+    sib_send, sib_recv, hop_send, left_recv, right_recv, half_send, half_recv,
+    cent_send, cent_recv, out_sem,
+):
+    me = lax.axis_index("seq")
+    core = lax.axis_index("dp")
+    other = 1 - core
+    scale = width ** (-0.5)
+    peers = [lax.rem(me + step, sources) for step in range(1, sources)]
+    my_rows = pl.ds(pl.multiple_of(me * tokens, tokens), tokens)
+    my_cols = pl.ds(pl.multiple_of(me * width, width), width)
+    stream = (queries, keys, values, grads)
+    half = model // sources // 2
+    every = sources * tokens
+
+    layer_in = pltpu.make_async_copy(layer, layer_rows, out_sem.at[0])
+    layer_in.start()
+    barrier = pltpu.get_barrier_semaphore()
+    for peer in peers:
+        pl.semaphore_signal(barrier, inc=1, device_id={"seq": peer}, device_id_type=MESH)
+    pl.semaphore_signal(barrier, inc=1, device_id={"dp": other}, device_id_type=MESH)
+    pl.semaphore_wait(barrier, sources)
+
+    def remote(src, dst, send, recv, target):
+        copy = pltpu.make_async_remote_copy(
+            src_ref=src, dst_ref=dst, send_sem=send, recv_sem=recv,
+            device_id=target, device_id_type=MESH,
+        )
+        copy.start()
+        return copy
+
+    id_copies = [
+        remote(ids.at[peer], ids_all.at[me], id_send.at[n], id_recv.at[n], {"seq": peer})
+        for n, peer in enumerate(peers)
+    ]
+    row_copies = []
+    for t in range(4):
+        copies = []
+        for n, peer in enumerate(peers):
+            cols = pl.ds(pl.multiple_of(peer * width, width), width)
+            copies.append(
+                remote(
+                    stream[t].at[:, cols], rows.at[t, my_rows, :],
+                    row_send.at[t, n], row_recv.at[t, n], {"seq": peer},
+                )
+            )
+        row_copies.append(copies)
+    local = [
+        pltpu.make_async_copy(stream[t].at[:, my_cols], rows.at[t, my_rows, :], local_sem.at[t])
+        for t in range(4)
+    ]
+    local.append(pltpu.make_async_copy(ids.at[me], ids_all.at[me], local_sem.at[4]))
+    for copy in local:
+        copy.start()
+
+    layer_in.wait()
+    piece = 256
+
+    def turn(n, carry):
+        cols = pl.ds(pl.multiple_of(n * piece, piece), piece)
+        layer_cols[cols, :] = layer_rows[:, cols].T
+        return carry
+
+    lax.fori_loop(0, model // piece, turn, 0)
+
+    local[4].wait()
+    for copy in id_copies:
+        copy.wait()
+    lane = lax.broadcasted_iota(jnp.int32, (128, 128), 1)
+    sub = lax.broadcasted_iota(jnp.int32, (128, 128), 0)
+    eye = jnp.where(lane == sub, 1.0, 0.0).astype(jnp.bfloat16)
+    inside = jnp.where(sub < clusters, 1.0, 0.0).astype(jnp.bfloat16)
+    level = lax.broadcasted_iota(jnp.int32, (128, tokens), 0).astype(jnp.float32)
+
+    for t in range(2):
+        local[t].wait()
+        for copy in row_copies[t]:
+            copy.wait()
+
+    def unit(array):
+        wide = array.astype(jnp.float32)
+        return wide * lax.rsqrt(jnp.mean(wide * wide, axis=-1, keepdims=True) + 1e-06)
+
+    cent = jnp.zeros((128, width), jnp.float32)
+    for s in range(sources):
+        span = slice(s * tokens, (s + 1) * tokens)
+        member = jnp.where(level == ids_all[s, 0:1, :], 1.0, 0.0).astype(jnp.bfloat16)
+        column = dot(member, eye, 0, 0)
+        keep[span, :] = dot(member, inside, 0, 0)
+        query_wide[span, :width] = rows[0, span, :]
+        key_wide[span, :width] = rows[1, span, :]
+        query_wide[span, width:] = column.astype(jnp.bfloat16)
+        key_wide[span, width:] = ((column - 1.0) * FAR).astype(jnp.bfloat16)
+        both = unit(rows[0, span, :]) + unit(rows[1, span, :])
+        high = both.astype(jnp.bfloat16)
+        low = (both - high.astype(jnp.float32)).astype(jnp.bfloat16)
+        cent = cent + dot(member, high, 1, 0) + dot(member, low, 1, 0)
+    cent_mine[...] = cent[: cent_mine.shape[0], :]
+    cent_first = remote(cent_mine, cent_sib, cent_send.at[0], cent_recv.at[0], {"dp": other})
+
+    chunk = probs.shape[2]
+    chunks = every // chunk
+
+    def soft(n, carry):
+        span = pl.ds(pl.multiple_of(n * chunk, chunk), chunk)
+        scores = dot(key_wide[...], query_wide[span, :], 1, 1)
+        top = jnp.max(scores, axis=0, keepdims=True)
+        weights = jnp.exp2((scores - top) * (scale * LOG2E))
+        probs[n] = weights * (1.0 / jnp.sum(weights, axis=0, keepdims=True))
+        return carry
+
+    lax.fori_loop(0, chunks, soft, 0)
+
+    cent_first.wait()
+    cent_all[me] = cent_mine[...] + cent_sib[...]
+    cent_copies = [
+        remote(
+            cent_all.at[me], cent_all.at[me], cent_send.at[n + 1], cent_recv.at[n + 1],
+            {"seq": peer},
+        )
+        for n, peer in enumerate(peers)
+    ]
+    for t in range(2, 4):
+        local[t].wait()
+        for copy in row_copies[t]:
+            copy.wait()
+    key_sum[...] = jnp.zeros_like(key_sum)
+    value_sum[...] = jnp.zeros_like(value_sum)
+
+    def backward(n, carry):
+        span = pl.ds(pl.multiple_of(n * chunk, chunk), chunk)
+        query = rows[0, span, :]
+        grad = rows[3, span, :]
+        share = probs[n]
+        share_low = share.astype(jnp.bfloat16)
+        dprobs = dot(rows[2], grad, 1, 1)
+        delta = jnp.sum(share_low.astype(jnp.float32) * dprobs, axis=0, keepdims=True)
+        dscores = (share * (dprobs - delta)).astype(jnp.bfloat16)
+        value_sum[...] += dot(share_low, grad, 1, 0)
+        key_sum[...] += dot(dscores, query, 1, 0)
+        query_part = dot(dscores, rows[1], 0, 0)
+        back[0, span, :] = (query_part * (keep[span, :] * scale)).astype(jnp.bfloat16)
+        return carry
+
+    lax.fori_loop(0, chunks, backward, 0)
+    back[1] = (key_sum[...] * (keep[...] * scale)).astype(jnp.bfloat16)
+    back[2] = (value_sum[...] * keep[...]).astype(jnp.bfloat16)
+
+    back_copies = []
+    for t in range(3):
+        copies = []
+        for n, peer in enumerate(peers):
+            span = pl.ds(pl.multiple_of(peer * tokens, tokens), tokens)
+            copies.append(
+                remote(
+                    back.at[t, span, :], landed.at[t, :, my_cols],
+                    back_send.at[t, n], back_recv.at[t, n], {"seq": peer},
+                )
+            )
+        back_copies.append(copies)
+        landed[t, :, my_cols] = back[t, my_rows, :]
+
+    outs = []
+    for t, out in enumerate((query_out, key_out, value_out)):
+        for copy in back_copies[t]:
+            copy.wait()
+        outs.append(pltpu.make_async_copy(landed.at[t], out, out_sem.at[t + 1]))
+        outs[-1].start()
+
+    def part(d, side, t):
+        span = pl.ds(pl.multiple_of(d * (2 * half) + side * half, half), half)
+        return dot(layer_cols[span, :], landed[t], 1, 0).astype(jnp.bfloat16)
+
+    low_first = jnp.where(me < sources // 2, 1, 0)
+    order = []
+    for k in range(sources // 2):
+        order.append(jnp.where(low_first == 1, sources - 1 - k, k))
+        order.append(jnp.where(low_first == 1, k, sources - 1 - k))
+
+    sib_copies = []
+    for d in order:
+        for t in range(3):
+            sib_term[d, t] = part(d, other, t)
+        sib_copies.append(
+            remote(sib_term.at[d], sib_in.at[d], sib_send.at[d], sib_recv.at[d], {"dp": other})
+        )
+    for d in order:
+        for t in range(3):
+            term[d, t] = part(d, core, t)
+
+    def add(d, arrived):
+        for t in range(3):
+            term[d, t] = (
+                term[d, t].astype(jnp.float32) + arrived[d, t].astype(jnp.float32)
+            ).astype(jnp.bfloat16)
+
+    def hop(d, side):
+        if side > 0:
+            return pltpu.make_async_remote_copy(
+                src_ref=term.at[d], dst_ref=from_left.at[d], send_sem=hop_send.at[d],
+                recv_sem=left_recv.at[d], device_id={"seq": me + 1}, device_id_type=MESH,
+            )
+        return pltpu.make_async_remote_copy(
+            src_ref=term.at[d], dst_ref=from_right.at[d], send_sem=hop_send.at[d],
+            recv_sem=right_recv.at[d], device_id={"seq": me - 1}, device_id_type=MESH,
+        )
+
+    last = sources - 1
+    for k, d in enumerate(order):
+        sib_copies[k].wait_recv()
+        add(d, sib_in)
+
+        @pl.when(jnp.logical_and(me < d, me > 0))
+        def _():
+            hop(d, 1).wait_recv()
+            add(d, from_left)
+
+        @pl.when(jnp.logical_and(me > d, me < last))
+        def _():
+            hop(d, -1).wait_recv()
+            add(d, from_right)
+
+        @pl.when(me < d)
+        def _():
+            hop(d, 1).start()
+
+        @pl.when(me > d)
+        def _():
+            hop(d, -1).start()
+
+    for t in range(3):
+        total[core, t] = term[me, t].astype(jnp.float32)
+
+    @pl.when(me > 0)
+    def _():
+        hop(me, 1).wait_recv()
+        for t in range(3):
+            total[core, t] += from_left[me, t].astype(jnp.float32)
+
+    @pl.when(me < last)
+    def _():
+        hop(me, -1).wait_recv()
+        for t in range(3):
+            total[core, t] += from_right[me, t].astype(jnp.float32)
+
+    final = remote(total.at[core], total.at[core], half_send, half_recv, {"dp": other})
+    for copy in cent_copies:
+        copy.wait()
+    sums = [cent_all[h, pl.ds(me, 1), :] for h in range(sources)]
+    sums = jnp.concatenate(sums, axis=0)
+    dirs_out[...] = sums * lax.rsqrt(jnp.mean(sums * sums, axis=-1, keepdims=True) + 1e-06)
+    for k, d in enumerate(order):
+        sib_copies[k].wait_send()
+
+        @pl.when(me < d)
+        def _():
+            hop(d, 1).wait_send()
+
+        @pl.when(me > d)
+        def _():
+            hop(d, -1).wait_send()
+
+    def store(side, sem):
+        for t in range(3):
+            copy = pltpu.make_async_copy(
+                total.at[side, t],
+                weight_out.at[t, pl.ds(pl.multiple_of(side * half, half), half), :],
+                out_sem.at[sem + t],
+            )
+            copy.start()
+            outs.append(copy)
+
+    store(core, 4)
+    final.wait()
+    store(other, 7)
+    for copy in outs:
+        copy.wait()
+
+
+def by_head(layer_input, queries, keys, values, out_grad, cluster_ids, slots, counts):
+    sources = lax.axis_size("seq")
+    heads_here = cluster_ids.shape[1]
+    tokens = queries.shape[1]
+    width = queries.shape[2] // heads_here
+    model = layer_input.shape[2]
+    clusters = sources * counts.shape[2]
+    every = sources * tokens
+    half = model // sources // 2
+    cols = heads_here * width
+    chunk = 256
+    low, wide = jnp.bfloat16, jnp.float32
+    ids = jnp.where(slots[0] >= 0, cluster_ids[0], clusters).astype(wide)
+    ids = jnp.broadcast_to(ids[:, None, :], (heads_here, 8, tokens))
+    anywhere = pl.BlockSpec(memory_space=pl.ANY)
+    dma = pltpu.SemaphoreType.DMA
+    token_grad = jax.ShapeDtypeStruct((tokens, cols), low)
+    query_grad, key_grad, value_grad, weight, dirs = pl.pallas_call(
+        functools.partial(exchange, sources, tokens, width, model, clusters),
+        out_shape=(
+            token_grad, token_grad, token_grad,
+            jax.ShapeDtypeStruct((3, model // sources, cols), wide),
+            jax.ShapeDtypeStruct((heads_here, width), wide),
+        ),
+        in_specs=[anywhere] * 6,
+        out_specs=(anywhere,) * 4 + (pl.BlockSpec(memory_space=pltpu.VMEM),),
+        scratch_shapes=[
+            pltpu.VMEM((4, every, width), low),
+            pltpu.VMEM((sources, 8, tokens), wide),
+            pltpu.VMEM((every, 2 * width), low),
+            pltpu.VMEM((every, 2 * width), low),
+            pltpu.VMEM((every, width), wide),
+            pltpu.VMEM((every // chunk, every, chunk), wide),
+            pltpu.VMEM((every, width), wide),
+            pltpu.VMEM((every, width), wide),
+            pltpu.VMEM((3, every, width), low),
+            pltpu.VMEM((3, tokens, cols), low),
+            pltpu.VMEM((tokens, model), low),
+            pltpu.VMEM((model, tokens), low),
+            pltpu.VMEM((sources, 3, half, cols), low),
+            pltpu.VMEM((sources, 3, half, cols), low),
+            pltpu.VMEM((sources, 3, half, cols), low),
+            pltpu.VMEM((sources, 3, half, cols), low),
+            pltpu.VMEM((sources, 3, half, cols), low),
+            pltpu.VMEM((2, 3, half, cols), wide),
+            pltpu.VMEM((8, width), wide),
+            pltpu.VMEM((8, width), wide),
+            pltpu.VMEM((sources, 8, width), wide),
+            dma((4, sources - 1)), dma((4, sources - 1)),
+            dma((sources - 1,)), dma((sources - 1,)), dma((5,)),
+            dma((3, sources - 1)), dma((3, sources - 1)),
+            dma((sources,)), dma((sources,)),
+            dma((sources,)), dma((sources,)), dma((sources,)),
+            dma, dma,
+            dma((sources,)), dma((sources,)), dma((10,)),
+        ],
+        compiler_params=pltpu.CompilerParams(
+            collective_id=0, has_side_effects=True, vmem_limit_bytes=60 * 1024 * 1024
+        ),
+    )(layer_input[0], queries[0], keys[0], values[0], out_grad[0], ids)
+    return (
+        query_grad[None], key_grad[None], value_grad[None],
+        weight.transpose(1, 0, 2), dirs[:, None, :],
+    )
 
 
 def for_sending(value):
@@ -59,7 +424,7 @@
     )
 
 
-def on_device(layer_input, queries, keys, values, out_grad, cluster_ids, slots, counts):
+def by_cluster(layer_input, queries, keys, values, out_grad, cluster_ids, slots, counts):
     sources = lax.axis_size("seq")
     heads_here = cluster_ids.shape[1]
     tokens_here = queries.shape[1]
@@ -155,6 +520,14 @@
     return (query_grad[None], key_grad[None], value_grad[None], weight_grad, centroid_dirs)
 
 
+def on_device(*arrays):
+    cluster_ids, counts = arrays[5], arrays[7]
+    sources = lax.axis_size("seq")
+    if cluster_ids.shape[1] == sources and counts.shape[2] == 1 and sources <= 8:
+        return by_head(*arrays)
+    return by_cluster(*arrays)
+
+
 def solution(mesh):
     return jax.shard_map(
         on_device,

time: 493 us -> 173 us (0.35)
  waiting for transfers between devices: 275 us -> 0 us
  Pallas kernels: 0 us -> 162 us
  local copies, waits for them, and re-layouts: 123 us -> 8.64 us
  matrix products: 30.6 us -> 0 us
  other arithmetic: 23.3 us -> 0.72 us
  between operations: 14.3 us -> 0.65 us
  blocking collectives: 13.4 us -> 0 us
  starting transfers between devices: 11.4 us -> 0 us
    all_to_all x2 -> x0, waiting for transfers between devices: 163 us -> none  [the longest x1 93.5 us: on_device(): lax.all_to_all(outgoing, 'seq', split_axis=1, concat_axis=1, tiled=True)]
    pallas_call x0 -> x1, Pallas kernels: none -> 162 us  [by_head(): pl.pallas_call(functools.partial(exchange, sources, tokens, width, model,...]
    reduce_scatter x1 -> x0, waiting for transfers between devices: 111 us -> none  [on_device(): lax.psum_scatter(contract_rows(inputs, stacked).reshape(lax.axis_size('se...]
    gather x1 -> x0, local copies, waits for them, and re-layouts: 41.5 us -> none  [on_device(): back = jax.vmap(lambda table, spots: table[spots])(padded, place)]
    dot_general x50 -> x0, matrix products: 30.6 us -> none  [the longest x17 13 us: contract_rows(): lax.dot_general(left, right, (((0,), (0,)), ((), ())), preferred_element_...]
    unnamed x32 -> x9, local copies, waits for them, and re-layouts: 34.2 us -> 8 us
    another operation x6 -> x0, local copies, waits for them, and re-layouts: 19.7 us -> none  [the longest x1 7.47 us: on_device(): blocks.transpose(0, 2, 1, 3, 4)]
    all_to_all x2 -> x0, starting transfers between devices: 11.1 us -> none  [the longest x1 6.45 us: on_device(): lax.all_to_all(outgoing, 'seq', split_axis=1, concat_axis=1, tiled=True)]
  transfers between devices with their start and end apart: 4 -> 0, of which waited for: 4 -> 0; matrix products, arithmetic and copies ran while one was open for 2% -> 0% of each run, Pallas kernels for 0% -> 0%
where the time goes in v1:
time: 173 us; the launch traced here: 172 us
  Pallas kernels  162 us (94%)
  local copies, waits for them, and re-layouts  8.64 us (5%)
    pallas_call x1, Pallas kernels, by_head(): pl.pallas_call(functools.partial(exchange, sources, tokens, width, model,...  162 us
    unnamed x9, local copies, waits for them, and re-layouts  8 us

profile of v1, /device:TPU:0, one launch (start us, length us, event | category | flops | bytes accessed | tf_op | source)
XLA Modules:
  0.0 172.4 jit_solution(4400544608707800455)
XLA Ops:
  0.6 0.7 convert_bitcast_fusion
  1.4 0.6 broadcast_in_dim.23.ids
  2.0 162.4 %shard_map.110 = (bf16[512,512]{1,0:T(8,128)(2,1)}, bf16[512,512]{1,0:T(8,128)(2,1)}, bf16[512,512]{1,0:T(8,128)(2,1)}, f32[3,512,512]{2,1,0:T(8,128)}, f32[4,128]{1,0:T(4,128)}) custom-call(bf16[512,2048]{1,0:T(8,128)(2,1)} %bitcast.15, bf16[512,512]{1,0:T(8,128)(2,1)} %bitcast.19, bf16[512,512]{1,0:T(8,128)(2,1)} %bitcast.20, bf16[512,512]{1,0:T(8,128)(2,1)} %bitcast.21, ...), custom_call_target="tpu_custom_call" | custom-call | tf_op jit(solution)/shard_map/pallas_call | solution.py:325
  164.4 0.0 copy-start
  164.4 2.0 %copy.18 = bf16[1,512,512]{2,1,0:T(8,128)(2,1)} copy(bf16[1,512,512]{2,1,0:T(8,128)(2,1)} %bitcast.18) | data formatting | bytes 1048576
  166.4 1.9 %copy.19 = bf16[1,512,512]{2,1,0:T(8,128)(2,1)} copy(bf16[1,512,512]{2,1,0:T(8,128)(2,1)} %bitcast.17) | data formatting | bytes 1048576
  168.2 1.9 %copy.20 = bf16[1,512,512]{2,1,0:T(8,128)(2,1)} copy(bf16[1,512,512]{2,1,0:T(8,128)(2,1)} %bitcast.16) | data formatting | bytes 1048576
  170.1 0.0 copy-done
  170.1 0.0 copy-start.1
  170.1 1.7 copy.21
  171.8 0.0 copy-done.1
  171.8 0.6 copy.22
Async XLA Ops:
  164.4 5.8 %copy-start = (f32[3,512,512]{2,1,0:T(8,128)S(1)}, f32[3,512,512]{2,1,0:T(8,128)}, u32[]{:S(2)}) copy-start(f32[3,512,512]{2,1,0:T(8,128)} %get-tuple-element.13) | copy-start | bytes 9437188
  170.1 1.7 copy-start.1

commit v2 on v1

--- a/solution.py
+++ b/solution.py
@@ -23,12 +23,12 @@
     sources, tokens, width, model, clusters,
     layer, queries, keys, values, grads, ids,
     query_out, key_out, value_out, weight_out, dirs_out,
-    rows, ids_all, query_wide, key_wide, keep, probs, key_sum, value_sum, back, landed,
+    rows, ids_all, query_wide, key_wide, keep, probs, key_sum, back, landed,
     layer_rows, layer_cols, sib_term, sib_in, term, from_left, from_right, total,
     cent_mine, cent_sib, cent_all,
     row_send, row_recv, id_send, id_recv, local_sem, back_send, back_recv,
     sib_send, sib_recv, hop_send, left_recv, right_recv, half_send, half_recv,
-    cent_send, cent_recv, out_sem,
+    cent_send, cent_recv, out_sem, store_sem,
 ):
     me = lax.axis_index("seq")
     core = lax.axis_index("dp")
@@ -61,8 +61,8 @@
         remote(ids.at[peer], ids_all.at[me], id_send.at[n], id_recv.at[n], {"seq": peer})
         for n, peer in enumerate(peers)
     ]
-    row_copies = []
-    for t in range(4):
+    row_copies = [None] * 4
+    for t in (0, 1, 3, 2):
         copies = []
         for n, peer in enumerate(peers):
             cols = pl.ds(pl.multiple_of(peer * width, width), width)
@@ -72,7 +72,7 @@
                     row_send.at[t, n], row_recv.at[t, n], {"seq": peer},
                 )
             )
-        row_copies.append(copies)
+        row_copies[t] = copies
     local = [
         pltpu.make_async_copy(stream[t].at[:, my_cols], rows.at[t, my_rows, :], local_sem.at[t])
         for t in range(4)
@@ -148,160 +148,209 @@
         )
         for n, peer in enumerate(peers)
     ]
-    for t in range(2, 4):
+    def give_back(t, step, peer):
+        span = pl.ds(pl.multiple_of(peer * tokens, tokens), tokens)
+        return pltpu.make_async_remote_copy(
+            src_ref=back.at[t, span, :], dst_ref=landed.at[t, :, my_cols],
+            send_sem=back_send.at[t, step], recv_sem=back_recv.at[t, step],
+            device_id={"seq": peer}, device_id_type=MESH,
+        )
+
+    def arrive(t):
         local[t].wait()
         for copy in row_copies[t]:
             copy.wait()
+
+    arrive(3)
+    for step in range(sources):
+        source = peers[step] if step < sources - 1 else me
+        span = pl.ds(pl.multiple_of(source * tokens, tokens), tokens)
+        gathered = jnp.zeros((tokens, width), jnp.float32)
+        for n in range(chunks):
+            gathered = gathered + dot(
+                probs[n, span, :].astype(jnp.bfloat16), rows[3, n * chunk : (n + 1) * chunk, :], 1, 0
+            )
+        back[2, span, :] = (gathered * keep[span, :]).astype(jnp.bfloat16)
+        if step < sources - 1:
+            give_back(2, step, source).start()
+        else:
+            landed[2, :, my_cols] = back[2, span, :]
+
+    arrive(2)
     key_sum[...] = jnp.zeros_like(key_sum)
-    value_sum[...] = jnp.zeros_like(value_sum)
-
-    def backward(n, carry):
+    each = tokens // chunk
+
+    def backward(index, carry):
+        step = index // each
+        source = lax.rem(me + 1 + step, sources)
+        n = source * each + lax.rem(index, each)
         span = pl.ds(pl.multiple_of(n * chunk, chunk), chunk)
-        query = rows[0, span, :]
-        grad = rows[3, span, :]
         share = probs[n]
         share_low = share.astype(jnp.bfloat16)
-        dprobs = dot(rows[2], grad, 1, 1)
+        dprobs = dot(rows[2], rows[3, span, :], 1, 1)
         delta = jnp.sum(share_low.astype(jnp.float32) * dprobs, axis=0, keepdims=True)
         dscores = (share * (dprobs - delta)).astype(jnp.bfloat16)
-        value_sum[...] += dot(share_low, grad, 1, 0)
-        key_sum[...] += dot(dscores, query, 1, 0)
         query_part = dot(dscores, rows[1], 0, 0)
         back[0, span, :] = (query_part * (keep[span, :] * scale)).astype(jnp.bfloat16)
+        key_sum[...] += dot(dscores, rows[0, span, :], 1, 0)
+
+        @pl.when(jnp.logical_and(lax.rem(index, each) == each - 1, step < sources - 1))
+        def _():
+            give_back(0, step, source).start()
+
         return carry
 
     lax.fori_loop(0, chunks, backward, 0)
+    landed[0, :, my_cols] = back[0, my_rows, :]
     back[1] = (key_sum[...] * (keep[...] * scale)).astype(jnp.bfloat16)
-    back[2] = (value_sum[...] * keep[...]).astype(jnp.bfloat16)
-
-    back_copies = []
-    for t in range(3):
-        copies = []
-        for n, peer in enumerate(peers):
-            span = pl.ds(pl.multiple_of(peer * tokens, tokens), tokens)
-            copies.append(
-                remote(
-                    back.at[t, span, :], landed.at[t, :, my_cols],
-                    back_send.at[t, n], back_recv.at[t, n], {"seq": peer},
-                )
-            )
-        back_copies.append(copies)
-        landed[t, :, my_cols] = back[t, my_rows, :]
+    for step, peer in enumerate(peers):
+        give_back(1, step, peer).start()
+    landed[1, :, my_cols] = back[1, my_rows, :]
 
     outs = []
-    for t, out in enumerate((query_out, key_out, value_out)):
-        for copy in back_copies[t]:
-            copy.wait()
-        outs.append(pltpu.make_async_copy(landed.at[t], out, out_sem.at[t + 1]))
-        outs[-1].start()
+
+    def collect(t):
+        for step, peer in enumerate(peers):
+            give_back(t, step, peer).wait()
+        copy = pltpu.make_async_copy(
+            landed.at[t], (query_out, key_out, value_out)[t], out_sem.at[t + 1]
+        )
+        copy.start()
+        outs.append(copy)
+
+    near_start = me < sources // 2
+    order = []
+    for k in range(sources // 2):
+        order.append(jnp.where(near_start, sources - 1 - k, k))
+        order.append(jnp.where(near_start, k, sources - 1 - k))
 
     def part(d, side, t):
         span = pl.ds(pl.multiple_of(d * (2 * half) + side * half, half), half)
         return dot(layer_cols[span, :], landed[t], 1, 0).astype(jnp.bfloat16)
 
-    low_first = jnp.where(me < sources // 2, 1, 0)
-    order = []
-    for k in range(sources // 2):
-        order.append(jnp.where(low_first == 1, sources - 1 - k, k))
-        order.append(jnp.where(low_first == 1, k, sources - 1 - k))
-
-    sib_copies = []
-    for d in order:
-        for t in range(3):
+    def across(t, d):
+        return pltpu.make_async_remote_copy(
+            src_ref=sib_term.at[d, t], dst_ref=sib_in.at[d, t],
+            send_sem=sib_send.at[d, t], recv_sem=sib_recv.at[d, t],
+            device_id={"dp": other}, device_id_type=MESH,
+        )
+
+    def terms(t):
+        collect(t)
+        for d in order:
             sib_term[d, t] = part(d, other, t)
-        sib_copies.append(
-            remote(sib_term.at[d], sib_in.at[d], sib_send.at[d], sib_recv.at[d], {"dp": other})
-        )
-    for d in order:
-        for t in range(3):
+            across(t, d).start()
+        for d in order:
             term[d, t] = part(d, core, t)
 
-    def add(d, arrived):
-        for t in range(3):
-            term[d, t] = (
-                term[d, t].astype(jnp.float32) + arrived[d, t].astype(jnp.float32)
-            ).astype(jnp.bfloat16)
-
-    def hop(d, side):
-        if side > 0:
-            return pltpu.make_async_remote_copy(
-                src_ref=term.at[d], dst_ref=from_left.at[d], send_sem=hop_send.at[d],
-                recv_sem=left_recv.at[d], device_id={"seq": me + 1}, device_id_type=MESH,
-            )
+    def hop(t, d, side):
+        landing, arrival = (from_left, left_recv) if side > 0 else (from_right, right_recv)
         return pltpu.make_async_remote_copy(
-            src_ref=term.at[d], dst_ref=from_right.at[d], send_sem=hop_send.at[d],
-            recv_sem=right_recv.at[d], device_id={"seq": me - 1}, device_id_type=MESH,
+            src_ref=term.at[d, t], dst_ref=landing.at[d, t],
+            send_sem=hop_send.at[d, t], recv_sem=arrival.at[d, t],
+            device_id={"seq": me + side}, device_id_type=MESH,
         )
 
     last = sources - 1
-    for k, d in enumerate(order):
-        sib_copies[k].wait_recv()
-        add(d, sib_in)
-
-        @pl.when(jnp.logical_and(me < d, me > 0))
+
+    def add(t, d, arrived):
+        term[d, t] = (
+            term[d, t].astype(jnp.float32) + arrived[d, t].astype(jnp.float32)
+        ).astype(jnp.bfloat16)
+
+    def hops(t):
+        for d in order:
+            across(t, d).wait_recv()
+            add(t, d, sib_in)
+
+            @pl.when(jnp.logical_and(me < d, me > 0))
+            def _():
+                hop(t, d, 1).wait_recv()
+                add(t, d, from_left)
+
+            @pl.when(jnp.logical_and(me > d, me < last))
+            def _():
+                hop(t, d, -1).wait_recv()
+                add(t, d, from_right)
+
+            @pl.when(me < d)
+            def _():
+                hop(t, d, 1).start()
+
+            @pl.when(me > d)
+            def _():
+                hop(t, d, -1).start()
+
+    def store(side, t):
+        copy = pltpu.make_async_copy(
+            total.at[side, t],
+            weight_out.at[t, pl.ds(pl.multiple_of(side * half, half), half), :],
+            store_sem.at[side, t],
+        )
+        copy.start()
+        outs.append(copy)
+
+    finals = {}
+
+    def finish(t):
+        total[core, t] = term[me, t].astype(jnp.float32)
+
+        @pl.when(me > 0)
         def _():
-            hop(d, 1).wait_recv()
-            add(d, from_left)
-
-        @pl.when(jnp.logical_and(me > d, me < last))
+            hop(t, me, 1).wait_recv()
+            total[core, t] += from_left[me, t].astype(jnp.float32)
+
+        @pl.when(me < last)
         def _():
-            hop(d, -1).wait_recv()
-            add(d, from_right)
-
-        @pl.when(me < d)
-        def _():
-            hop(d, 1).start()
-
-        @pl.when(me > d)
-        def _():
-            hop(d, -1).start()
-
-    for t in range(3):
-        total[core, t] = term[me, t].astype(jnp.float32)
-
-    @pl.when(me > 0)
-    def _():
-        hop(me, 1).wait_recv()
-        for t in range(3):
-            total[core, t] += from_left[me, t].astype(jnp.float32)
-
-    @pl.when(me < last)
-    def _():
-        hop(me, -1).wait_recv()
-        for t in range(3):
+            hop(t, me, -1).wait_recv()
             total[core, t] += from_right[me, t].astype(jnp.float32)
 
-    final = remote(total.at[core], total.at[core], half_send, half_recv, {"dp": other})
+        finals[t] = remote(
+            total.at[core, t], total.at[core, t], half_send.at[t], half_recv.at[t], {"dp": other}
+        )
+        store(core, t)
+
+    terms(2)
+    terms(0)
+    hops(2)
+    terms(1)
+    hops(0)
+    finish(2)
+    hops(1)
+    finish(0)
     for copy in cent_copies:
         copy.wait()
     sums = [cent_all[h, pl.ds(me, 1), :] for h in range(sources)]
     sums = jnp.concatenate(sums, axis=0)
     dirs_out[...] = sums * lax.rsqrt(jnp.mean(sums * sums, axis=-1, keepdims=True) + 1e-06)
-    for k, d in enumerate(order):
-        sib_copies[k].wait_send()
-
-        @pl.when(me < d)
-        def _():
-            hop(d, 1).wait_send()
-
-        @pl.when(me > d)
-        def _():
-            hop(d, -1).wait_send()
-
-    def store(side, sem):
-        for t in range(3):
-            copy = pltpu.make_async_copy(
-                total.at[side, t],
-                weight_out.at[t, pl.ds(pl.multiple_of(side * half, half), half), :],
-                out_sem.at[sem + t],
-            )
-            copy.start()
-            outs.append(copy)
-
-    store(core, 4)
-    final.wait()
-    store(other, 7)
+    finish(1)
+    for t in (2, 0, 1):
+        for d in order:
+            across(t, d).wait_send()
+
+            @pl.when(me < d)
+            def _():
+                hop(t, d, 1).wait_send()
+
+            @pl.when(me > d)
+            def _():
+                hop(t, d, -1).wait_send()
+
+    for t in (2, 0, 1):
+        finals[t].wait()
+        store(other, t)
     for copy in outs:
+        copy.wait()
+
+
+def settle(*refs):
+    count = len(refs) // 2
+    copies = [
+        pltpu.make_async_copy(refs[i], refs[count + i], refs[-1].at[i]) for i in range(count)
+    ]
+    for copy in copies:
+        copy.start()
+    for copy in copies:
         copy.wait()
 
 
@@ -322,7 +371,7 @@
     anywhere = pl.BlockSpec(memory_space=pl.ANY)
     dma = pltpu.SemaphoreType.DMA
     token_grad = jax.ShapeDtypeStruct((tokens, cols), low)
-    query_grad, key_grad, value_grad, weight, dirs = pl.pallas_call(
+    results = pl.pallas_call(
         functools.partial(exchange, sources, tokens, width, model, clusters),
         out_shape=(
             token_grad, token_grad, token_grad,
@@ -338,7 +387,6 @@
             pltpu.VMEM((every, 2 * width), low),
             pltpu.VMEM((every, width), wide),
             pltpu.VMEM((every // chunk, every, chunk), wide),
-            pltpu.VMEM((every, width), wide),
             pltpu.VMEM((every, width), wide),
             pltpu.VMEM((3, every, width), low),
             pltpu.VMEM((3, tokens, cols), low),
@@ -356,15 +404,22 @@
             dma((4, sources - 1)), dma((4, sources - 1)),
             dma((sources - 1,)), dma((sources - 1,)), dma((5,)),
             dma((3, sources - 1)), dma((3, sources - 1)),
-            dma((sources,)), dma((sources,)),
-            dma((sources,)), dma((sources,)), dma((sources,)),
-            dma, dma,
-            dma((sources,)), dma((sources,)), dma((10,)),
+            dma((sources, 3)), dma((sources, 3)),
+            dma((sources, 3)), dma((sources, 3)), dma((sources, 3)),
+            dma((3,)), dma((3,)),
+            dma((sources,)), dma((sources,)), dma((4,)), dma((2, 3)),
         ],
         compiler_params=pltpu.CompilerParams(
             collective_id=0, has_side_effects=True, vmem_limit_bytes=60 * 1024 * 1024
         ),
     )(layer_input[0], queries[0], keys[0], values[0], out_grad[0], ids)
+    query_grad, key_grad, value_grad, weight, dirs = pl.pallas_call(
+        settle,
+        out_shape=tuple(jax.ShapeDtypeStruct(a.shape, a.dtype) for a in results),
+        in_specs=[anywhere] * 5,
+        out_specs=(anywhere,) * 5,
+        scratch_shapes=[dma((5,))],
+    )(*results)
     return (
         query_grad[None], key_grad[None], value_grad[None],
         weight.transpose(1, 0, 2), dirs[:, None, :],

time: 173 us -> 290 us (1.68)
  Pallas kernels: 162 us -> 288 us
  local copies, waits for them, and re-layouts: 8.64 us -> 0.63 us
    pallas_call x0 -> x1, Pallas kernels: none -> 144 us  [by_head(): pl.pallas_call(settle, out_shape=tuple((jax.ShapeDtypeStruct(a.shape, a.d...]
    pallas_call x1, Pallas kernels: 162 us -> 144 us  [by_head(): pl.pallas_call(functools.partial(exchange, sources, tokens, width, model,...]
    unnamed x9 -> x0, local copies, waits for them, and re-layouts: 8 us -> none
where the time goes in v2:
time: 290 us
  Pallas kernels  288 us (99%)
    pallas_call x1, Pallas kernels, by_head(): pl.pallas_call(settle, out_shape=tuple((jax.ShapeDtypeStruct(a.shape, a.d...  144 us
    pallas_call x1, Pallas kernels, by_head(): pl.pallas_call(functools.partial(exchange, sources, tokens, width, model,...  144 us

profile of v2, /device:TPU:0, one launch (start us, length us, event | category | flops | bytes accessed | tf_op | source)
XLA Modules:
  0.0 289.8 jit_solution(6407015578218677543)
XLA Ops:
  0.6 0.7 convert_bitcast_fusion
  1.4 0.6 broadcast_in_dim.23.ids
  2.0 143.6 %shard_map.110 = (bf16[512,512]{1,0:T(8,128)(2,1)}, bf16[512,512]{1,0:T(8,128)(2,1)}, bf16[512,512]{1,0:T(8,128)(2,1)}, f32[3,512,512]{2,1,0:T(8,128)}, f32[4,128]{1,0:T(4,128)}) custom-call(bf16[512,2048]{1,0:T(8,128)(2,1)} %bitcast.14, bf16[512,512]{1,0:T(8,128)(2,1)} %bitcast.15, bf16[512,512]{1,0:T(8,128)(2,1)} %bitcast.16, bf16[512,512]{1,0:T(8,128)(2,1)} %bitcast.17, ...), custom_call_target="tpu_custom_call" | custom-call | tf_op jit(solution)/shard_map/pallas_call | solution.py:374
  145.6 144.2 %shard_map.111 = (bf16[512,512]{1,0:T(8,128)(2,1)}, bf16[512,512]{1,0:T(8,128)(2,1)}, bf16[512,512]{1,0:T(8,128)(2,1)}, f32[3,512,512]{2,1,0:T(8,128)}, f32[4,128]{1,0:T(4,128)}) custom-call(bf16[512,512]{1,0:T(8,128)(2,1)} %get-tuple-element.15.refs_0_, bf16[512,512]{1,0:T(8,128)(2,1)} %get-tuple-element.16.refs_1_, ...), custom_call_target="tpu_custom_call" | custom-call | tf_op jit(solution)/shard_map/pallas_call | solution.py:416

commit v3 on v2

--- a/solution.py
+++ b/solution.py
@@ -21,9 +21,9 @@
 
 def exchange(
     sources, tokens, width, model, clusters,
-    layer, queries, keys, values, grads, ids,
+    layer, queries, keys, values, grads, cluster, slot,
     query_out, key_out, value_out, weight_out, dirs_out,
-    rows, ids_all, query_wide, key_wide, keep, probs, key_sum, back, landed,
+    rows, ids, ids_all, query_wide, key_wide, keep, probs, key_sum, back, landed,
     layer_rows, layer_cols, sib_term, sib_in, term, from_left, from_right, total,
     cent_mine, cent_sib, cent_all,
     row_send, row_recv, id_send, id_recv, local_sem, back_send, back_recv,
@@ -41,6 +41,9 @@
     half = model // sources // 2
     every = sources * tokens
 
+    named = jnp.where(slot[...] >= 0, cluster[...], clusters).astype(jnp.float32)
+    for h in range(sources):
+        ids[h] = jnp.broadcast_to(named[h : h + 1, :], (8, tokens))
     layer_in = pltpu.make_async_copy(layer, layer_rows, out_sem.at[0])
     layer_in.start()
     barrier = pltpu.get_barrier_semaphore()
@@ -62,7 +65,8 @@
         for n, peer in enumerate(peers)
     ]
     row_copies = [None] * 4
-    for t in (0, 1, 3, 2):
+
+    def leave(t):
         copies = []
         for n, peer in enumerate(peers):
             cols = pl.ds(pl.multiple_of(peer * width, width), width)
@@ -73,6 +77,9 @@
                 )
             )
         row_copies[t] = copies
+
+    leave(0)
+    leave(1)
     local = [
         pltpu.make_async_copy(stream[t].at[:, my_cols], rows.at[t, my_rows, :], local_sem.at[t])
         for t in range(4)
@@ -101,9 +108,14 @@
     level = lax.broadcasted_iota(jnp.int32, (128, tokens), 0).astype(jnp.float32)
 
     for t in range(2):
+        for copy in row_copies[t]:
+            copy.wait_send()
+    leave(3)
+    leave(2)
+    for t in range(2):
         local[t].wait()
         for copy in row_copies[t]:
-            copy.wait()
+            copy.wait_recv()
 
     def unit(array):
         wide = array.astype(jnp.float32)
@@ -137,7 +149,13 @@
         probs[n] = weights * (1.0 / jnp.sum(weights, axis=0, keepdims=True))
         return carry
 
-    lax.fori_loop(0, chunks, soft, 0)
+    lax.fori_loop(0, chunks // 2, soft, 0)
+    for copy in row_copies[3]:
+        copy.wait_send()
+    lax.fori_loop(chunks // 2, chunks, soft, 0)
+    local[3].wait()
+    for copy in row_copies[3]:
+        copy.wait_recv()
 
     cent_first.wait()
     cent_all[me] = cent_mine[...] + cent_sib[...]
@@ -156,12 +174,6 @@
             device_id={"seq": peer}, device_id_type=MESH,
         )
 
-    def arrive(t):
-        local[t].wait()
-        for copy in row_copies[t]:
-            copy.wait()
-
-    arrive(3)
     for step in range(sources):
         source = peers[step] if step < sources - 1 else me
         span = pl.ds(pl.multiple_of(source * tokens, tokens), tokens)
@@ -176,7 +188,9 @@
         else:
             landed[2, :, my_cols] = back[2, span, :]
 
-    arrive(2)
+    local[2].wait()
+    for copy in row_copies[2]:
+        copy.wait()
     key_sum[...] = jnp.zeros_like(key_sum)
     each = tokens // chunk
 
@@ -344,13 +358,21 @@
 
 
 def settle(*refs):
-    count = len(refs) // 2
-    copies = [
-        pltpu.make_async_copy(refs[i], refs[count + i], refs[-1].at[i]) for i in range(count)
+    count = (len(refs) - 1) // 3
+    sem = refs[-1]
+    came = [
+        pltpu.make_async_copy(refs[i], refs[2 * count + i], sem.at[0, i]) for i in range(count)
     ]
-    for copy in copies:
+    went = [
+        pltpu.make_async_copy(refs[2 * count + i], refs[count + i], sem.at[1, i])
+        for i in range(count)
+    ]
+    for copy in came:
         copy.start()
-    for copy in copies:
+    for i in range(count):
+        came[i].wait()
+        went[i].start()
+    for copy in went:
         copy.wait()
 
 
@@ -366,8 +388,7 @@
     cols = heads_here * width
     chunk = 256
     low, wide = jnp.bfloat16, jnp.float32
-    ids = jnp.where(slots[0] >= 0, cluster_ids[0], clusters).astype(wide)
-    ids = jnp.broadcast_to(ids[:, None, :], (heads_here, 8, tokens))
+    inside = pl.BlockSpec(memory_space=pltpu.VMEM)
     anywhere = pl.BlockSpec(memory_space=pl.ANY)
     dma = pltpu.SemaphoreType.DMA
     token_grad = jax.ShapeDtypeStruct((tokens, cols), low)
@@ -378,10 +399,11 @@
             jax.ShapeDtypeStruct((3, model // sources, cols), wide),
             jax.ShapeDtypeStruct((heads_here, width), wide),
         ),
-        in_specs=[anywhere] * 6,
-        out_specs=(anywhere,) * 4 + (pl.BlockSpec(memory_space=pltpu.VMEM),),
+        in_specs=[anywhere] * 5 + [inside] * 2,
+        out_specs=(anywhere,) * 4 + (inside,),
         scratch_shapes=[
             pltpu.VMEM((4, every, width), low),
+            pltpu.VMEM((sources, 8, tokens), wide),
             pltpu.VMEM((sources, 8, tokens), wide),
             pltpu.VMEM((every, 2 * width), low),
             pltpu.VMEM((every, 2 * width), low),
@@ -412,13 +434,14 @@
         compiler_params=pltpu.CompilerParams(
             collective_id=0, has_side_effects=True, vmem_limit_bytes=60 * 1024 * 1024
         ),
-    )(layer_input[0], queries[0], keys[0], values[0], out_grad[0], ids)
+    )(layer_input[0], queries[0], keys[0], values[0], out_grad[0], cluster_ids[0], slots[0])
     query_grad, key_grad, value_grad, weight, dirs = pl.pallas_call(
         settle,
         out_shape=tuple(jax.ShapeDtypeStruct(a.shape, a.dtype) for a in results),
         in_specs=[anywhere] * 5,
         out_specs=(anywhere,) * 5,
-        scratch_shapes=[dma((5,))],
+        scratch_shapes=[pltpu.VMEM(a.shape, a.dtype) for a in results] + [dma((2, 5))],
+        compiler_params=pltpu.CompilerParams(vmem_limit_bytes=60 * 1024 * 1024),
     )(*results)
     return (
         query_grad[None], key_grad[None], value_grad[None],

time: 290 us -> 150 us (0.52)
  Pallas kernels: 288 us -> 149 us
    pallas_call x1, Pallas kernels: 144 us -> 4.7 us  [by_head(): pl.pallas_call(settle, out_shape=tuple((jax.ShapeDtypeStruct(a.shape, a.d...]
where the time goes in v3:
time: 150 us
  Pallas kernels  149 us (99%)
    pallas_call x1, Pallas kernels, by_head(): pl.pallas_call(functools.partial(exchange, sources, tokens, width, model,...  145 us
    pallas_call x1, Pallas kernels, by_head(): pl.pallas_call(settle, out_shape=tuple((jax.ShapeDtypeStruct(a.shape, a.d...  4.7 us

profile of v3, /device:TPU:0, one launch (start us, length us, event | category | flops | bytes accessed | tf_op | source)
XLA Modules:
  0.0 150.1 jit_solution(12237979190295875706)
XLA Ops:
  0.6 144.6 %shard_map.110 = (bf16[512,512]{1,0:T(8,128)(2,1)}, bf16[512,512]{1,0:T(8,128)(2,1)}, bf16[512,512]{1,0:T(8,128)(2,1)}, f32[3,512,512]{2,1,0:T(8,128)}, f32[4,128]{1,0:T(4,128)}) custom-call(bf16[512,2048]{1,0:T(8,128)(2,1)} %bitcast.14, bf16[512,512]{1,0:T(8,128)(2,1)} %bitcast.15, bf16[512,512]{1,0:T(8,128)(2,1)} %bitcast.16, bf16[512,512]{1,0:T(8,128)(2,1)} %bitcast.17, ...), custom_call_target="tpu_custom_call" | custom-call | tf_op jit(solution)/shard_map/pallas_call | solution.py:395
  145.3 4.7 %shard_map.111 = (bf16[512,512]{1,0:T(8,128)(2,1)}, bf16[512,512]{1,0:T(8,128)(2,1)}, bf16[512,512]{1,0:T(8,128)(2,1)}, f32[3,512,512]{2,1,0:T(8,128)}, f32[4,128]{1,0:T(4,128)}) custom-call(bf16[512,512]{1,0:T(8,128)(2,1)} %get-tuple-element.15.refs_0_, bf16[512,512]{1,0:T(8,128)(2,1)} %get-tuple-element.16.refs_1_, ...), custom_call_target="tpu_custom_call" | custom-call | tf_op jit(solution)/shard_map/pallas_call | solution.py:438
